TPU v7x, 768 devices: a whole 4x8x12 slice. The times are simulated.
768 devices in a mesh: dp: 12 (over z_hi, x), tensor: 64 (over y, z_lo, core).
Axes of the slice: x: 4, y: 8, z: 12 (z_hi: 3, z_lo: 4; z = z_hi * 4 + z_lo), core: 2. Of those that a mesh axis runs over, the one named last changes fastest.
Arguments:
- out_grad: bfloat16 [6144, 6144], P(('dp', 'tensor')), may hold values from -24 to 24
- normed: bfloat16 [6144, 8192], P('dp', 'tensor'), may hold values from -0.078125 to 0.078125
- w_out: bfloat16 [8192, 6144], P('tensor', 'dp'), may hold values from -0.078125 to 0.078125
Outputs:
- d_normed: bfloat16 [6144, 8192], P('dp', 'tensor')
- d_w_out: bfloat16 [8192, 6144], P('tensor', 'dp')
All inputs are finite; a program needn't handle non-finite values.
Results may differ from a plain program's by a relative error of at most 0.017.
Values may be sent and summed in bfloat16 or wider, within the bound.
A program may use at most 32 MiB of HBM per device.

v0:
```python
import jax
import jax.numpy as jnp
from jax import lax
from jax.sharding import PartitionSpec as P


def body(out_grad, normed, w_out):
    w_full = lax.all_gather(w_out, "dp", axis=1, tiled=True)
    gathered = lax.all_gather(out_grad, "tensor", axis=0, tiled=True)
    d_rows = lax.dot_general(
        gathered, w_full, (((1,), (1,)), ((), ())), preferred_element_type=jnp.float32
    )
    d_weight = lax.dot_general(
        normed, gathered, (((0,), (0,)), ((), ())), preferred_element_type=jnp.float32
    )
    d_shard = lax.psum_scatter(d_weight.astype(jnp.bfloat16), "dp", scatter_dimension=1, tiled=True)
    return (d_rows.astype(jnp.bfloat16), d_shard)


def solution(mesh):
    in_specs = (P(("dp", "tensor"), None), P("dp", "tensor"), P("tensor", "dp"))
    out_specs = (P("dp", "tensor"), P("tensor", "dp"))
    return jax.shard_map(body, mesh=mesh, in_specs=in_specs, out_specs=out_specs, check_vma=False)
```

profile of v0, /device:TPU:1, one launch (start us, length us, event | category | flops | bytes accessed | tf_op | source)
XLA Modules:
  0.0 411.3 jit_solution(5676032459553589454)
XLA Ops:
  7.2 0.0 copy-start
  7.2 0.0 all-gather.3.cloned.1.call-start
  7.2 0.7 all-gather.3.cloned.1.call-update
  7.9 0.0 all-gather.5.cloned.1.call-start
  8.0 0.7 all-gather.5.cloned.1.call-update
  8.7 0.0 reduce-scatter.2.cloned.1.call-start
  8.7 135.8 %all-gather.3.cloned.1.call-done = bf16[512,6144]{1,0:T(8,128)(2,1)} async-done(((bf16[8,6144]{1,0:T(8,128)(2,1)}), bf16[512,6144]{1,0:T(8,128)(2,1)}) %all-gather.3.cloned.1.call-update) | async-done | bytes 6291472 | tf_op jit(solution)/shard_map/all_gather | solution.py:9
  144.5 0.0 copy-done
  144.5 5.0 %convolution_convert_fusion = bf16[128,6144]{1,0:T(8,128)(2,1)} fusion(bf16[512,128]{1,0:T(8,128)(2,1)S(1)} %copy-done, bf16[512,6144]{1,0:T(8,128)(2,1)} %all-gather.3.cloned.1.call-done), kind=kOutput, calls=%fused_computation | convolution fusion | flops 806092800 | bytes 7995392 | tf_op jit(solution)/shard_map/dot_general | solution.py:13
  149.5 0.0 reduce-scatter.2.cloned.1.call-update
  149.6 82.2 %all-gather.5.cloned.1.call-done = bf16[128,6144]{1,0:T(8,128)(2,1)} async-done(((bf16[128,512]{1,0:T(8,128)(2,1)}), bf16[128,6144]{1,0:T(8,128)(2,1)}) %all-gather.5.cloned.1.call-update) | async-done | bytes 1572880 | tf_op jit(solution)/shard_map/all_gather | solution.py:8
  231.8 5.7 %convolution_convert_fusion.1 = bf16[512,128]{1,0:T(8,128)(2,1)} fusion(bf16[512,6144]{1,0:T(8,128)(2,1)} %all-gather.3.cloned.1.call-done, bf16[128,6144]{1,0:T(8,128)(2,1)} %all-gather.5.cloned.1.call-done), kind=kOutput, calls=%fused_computation.1 | convolution fusion | flops 805371904 | bytes 7995392 | tf_op jit(solution)/shard_map/dot_general | solution.py:10
  237.4 167.4 %reduce-scatter.2.cloned.1.call-done = bf16[128,512]{1,0:T(8,128)(2,1)} async-done(((bf16[128,6144]{1,0:T(8,128)(2,1)}), bf16[128,512]{1,0:T(8,128)(2,1)}) %reduce-scatter.2.cloned.1.call-update) | async-done | bytes 131088 | tf_op jit(solution)/shard_map/reduce_scatter | solution.py:16
Async XLA Ops:
  7.2 137.3 %copy-start = (bf16[512,128]{1,0:T(8,128)(2,1)S(1)}, bf16[512,128]{1,0:T(8,128)(2,1)}, u32[]{:S(2)}) copy-start(bf16[512,128]{1,0:T(8,128)(2,1)} %param.4) | copy-start | bytes 393220
  7.2 137.3 %all-gather.3.cloned.1.call-start = ((), (), s32[]{:S(2)}) async-start(), calls=%async_computation.1 | async-start | bytes 6389760 | tf_op jit(solution)/shard_map/all_gather | solution.py:9
  7.9 223.9 %all-gather.5.cloned.1.call-start = ((), (), s32[]{:S(2)}) async-start(), calls=%async_computation.2 | async-start | bytes 1703936 | tf_op jit(solution)/shard_map/all_gather | solution.py:8
  8.7 396.2 %reduce-scatter.2.cloned.1.call-start = ((), (), s32[]{:S(2)}) async-start(), calls=%async_computation.3 | async-start | bytes 1703936 | tf_op jit(solution)/shard_map/reduce_scatter | solution.py:16
Sparse Core Ops, SparseCore 0:
  10.5 133.9 all-gather.2
  148.4 83.3 all-gather.4
  237.6 167.1 reduce-scatter.1
where the time goes:
time: 411 us
  waiting for transfers between devices  387 us (94%)
  between operations  13.8 us (3%)
  matrix products  10.7 us (3%)
    reduce_scatter x1, waiting for transfers between devices, body(): lax.psum_scatter(d_weight.astype(jnp.bfloat16), 'dp', scatter_dimension=1...  167 us
    all_gather x1, waiting for transfers between devices, body(): gathered = lax.all_gather(out_grad, 'tensor', axis=0, tiled=True)  136 us
    all_gather x1, waiting for transfers between devices, body(): w_full = lax.all_gather(w_out, 'dp', axis=1, tiled=True)  82.2 us
  transfers between devices with their start and end apart: 3, of which 3 were waited for; matrix products, arithmetic and copies ran while one was open for 3% of the time, Pallas kernels for 0%

commit v1 on v0

v1 whole, which is shorter than its diff:
```python
import jax
import jax.numpy as jnp
from jax import lax
from jax.experimental import pallas as pl
from jax.experimental.pallas import tpu as pltpu
from jax.sharding import PartitionSpec as P

X, ZH, Y, ZL = 4, 3, 8, 4
R = 8
C = 128
K = 2 * ZH
KZ = 2 * (ZH - 1)
W = X * C
B = 2 * R * ZL
RT = B * Y
LS, SS = Y // 2, Y // 2 - 1
WLAG = 2
MESH = pl.DeviceIdType.MESH
BF, F32 = jnp.bfloat16, jnp.float32


def kernel(
    og_ref, n_ref, w_ref, dn_ref, dw_ref,
    og_par, og, nb, nt, w, part, rsx, zs, rsz, fin, finr, acc, dns, dnr,
    c_send, c_recv, zl_send, zl_recv, y_send, y_recv, wz_send, wz_recv, wx_send, wx_recv,
    rsx_send, rsx_recv, rsz_send, rsz_recv,
):
    dp, tn = lax.axis_index("dp"), lax.axis_index("tensor")
    zh, x = dp // X, dp % X
    y, zl, c = tn // (2 * ZL), (tn // 2) % ZL, tn % 2
    o = 1 - c
    partner = (dp, tn + 1 - 2 * c)
    zl_peer = [(dp, (y * ZL + (zl + j) % ZL) * 2 + c) for j in range(1, ZL)]
    x_peer = [(zh * X + (x + j) % X, tn) for j in range(1, X)]
    z_peer = [(((zh + j) % ZH) * X + x, tn) for j in range(1, ZH)]

    def y_peer(sign):
        return (dp, (((y + sign + Y) % Y) * ZL + zl) * 2 + c)

    def send(src, dst, ssem, rsem, to):
        pltpu.make_async_remote_copy(
            src_ref=src, dst_ref=dst, send_sem=ssem, recv_sem=rsem, device_id=to, device_id_type=MESH
        ).start()

    def wait(ref, sem):
        pltpu.make_async_copy(ref, ref, sem).wait()

    def rows(k, start, size):
        return pl.ds(pl.multiple_of(k * RT + start, 16), size)

    def block(k, at):
        return og.at[rows(k, ((at + 2 * Y) % Y) * B, B)]

    def way(k):
        return 1 - 2 * (k % 2)

    def send_long(k, s):
        b = block(k, y - way(k) * s)
        send(b, b, y_send.at[k], y_recv.at[k, s], y_peer(way(k)))

    def send_short(k, s):
        b = block(k, y + way(k) * s)
        send(b, b, y_send.at[k], y_recv.at[k, LS + s], y_peer(-way(k)))

    def wait_long(k, s):
        wait(block(k, y - way(k) * (s + 1)), y_recv.at[k, s])

    def wait_short(k, s):
        wait(block(k, y + way(k) * (s + 1)), y_recv.at[k, LS + s])

    def send_w(k):
        for j in range(1, X):
            send(w.at[k, 0], w.at[k, X - j], wx_send.at[k], wx_recv.at[k], x_peer[j - 1])

    def weight(k):
        chunk = og[rows(k, 0, RT), :]
        p = jnp.dot(nt[...], chunk, preferred_element_type=F32)
        for j in range(X):
            part[k, j] = p[:, j * C : (j + 1) * C].astype(BF)
        for j in range(1, X):
            send(part.at[k, j], rsx.at[k, j - 1], rsx_send.at[k], rsx_recv.at[k], x_peer[j - 1])

    def summed(k):
        wait(rsx.at[k], rsx_recv.at[k])
        total = part[k, 0].astype(F32)
        for j in range(X - 1):
            total = total + rsx[k, j].astype(F32)
        return total

    def normed_grad(k):
        wait(w.at[k, pl.ds(1, X - 1)], wx_recv.at[k])
        chunk = og[rows(k, 0, RT), :]
        wk = jnp.concatenate([w[k, j] for j in range(X)], axis=1)
        acc[...] += lax.dot_general(chunk, wk, (((1,), (1,)), ((), ())), preferred_element_type=F32)

    barrier = pltpu.get_barrier_semaphore()
    peers = [partner] + zl_peer + x_peer + z_peer + [y_peer(1), y_peer(-1)]
    for peer in peers:
        pl.semaphore_signal(barrier, inc=1, device_id=peer, device_id_type=MESH)
    pl.semaphore_wait(barrier, len(peers))

    send(og_ref, og_par, c_send.at[0], c_recv.at[0], partner)
    mine = pl.ds(pl.multiple_of(c * C, C), C)
    for h in range(2):
        cols = pl.ds(pl.multiple_of(o * 2 * C + h * C, C), C)
        send(w_ref.at[:, cols], w.at[KZ + h, 0, mine], c_send.at[1 + h], c_recv.at[1 + h], partner)
    send(n_ref, nb.at[c], c_send.at[3], c_recv.at[3], partner)
    for h in range(2):
        w[KZ + h, 0, mine, :] = w_ref[:, pl.ds(pl.multiple_of(c * 2 * C + h * C, C), C)]
    nb[c] = n_ref[...]
    acc[...] = jnp.zeros_like(acc)

    slab = (y * ZL + zl) * 2 * R
    wait(og_par, c_recv.at[0])

    def spread(k, carry):
        zt = (zh + 1 + k // 2) % ZH
        for j in range(X):
            col = (zt * X + (x + j) % X) * 4 * C + c * 2 * C + (k % 2) * C
            col = pl.ds(pl.multiple_of(col, C), C)
            a, b = og_ref[:, col].astype(F32), og_par[:, col].astype(F32)
            top, low = jnp.where(c == 0, a, b), jnp.where(c == 0, b, a)
            og[rows(k, slab, 2 * R), j * C : (j + 1) * C] = jnp.concatenate([top, low], axis=0).astype(BF)
        piece = og.at[rows(k, slab, 2 * R)]
        for peer in zl_peer:
            send(piece, piece, zl_send.at[k], zl_recv.at[k], peer)
        return carry

    lax.fori_loop(0, K, spread, 0)

    for h in range(2):
        theirs = pl.ds(pl.multiple_of(o * C, C), C)
        wait(w.at[KZ + h, 0, theirs], c_recv.at[1 + h])
        for j in range(1, ZH):
            k = 2 * (ZH - 1 - j) + h
            send(w.at[KZ + h, 0], w.at[k, 0], wz_send.at[k], wz_recv.at[k], z_peer[j - 1])
    for h in range(2):
        send_w(KZ + h)
    wait(nb.at[o], c_recv.at[3])
    for i in range(2):
        nt[i * C : (i + 1) * C, :] = nb[i].astype(F32).T.astype(BF)

    def slot(s, carry):
        @pl.when(s < K)
        def _():
            wait(og.at[rows(s, 0, B - 2 * R)], zl_recv.at[s])
            send_long(s, 0)
            send_short(s, 0)

        for i in range(1, LS):
            @pl.when((s >= i) & (s - i < K))
            def _():
                k = s - i
                wait_long(k, i - 1)
                send_long(k, i)
                if i < SS:
                    wait_short(k, i - 1)
                    send_short(k, i)

        @pl.when((s >= WLAG) & (s - WLAG < KZ))
        def _():
            k = s - WLAG
            wait(w.at[k, 0], wz_recv.at[k])
            send_w(k)

        @pl.when(s >= LS)
        def _():
            k = s - LS
            wait_long(k, LS - 1)
            wait_short(k, SS - 1)
            weight(k)

        @pl.when(s >= LS + 1)
        def _():
            k = s - LS - 1
            zs[k] = summed(k).astype(BF)
            for i in range(ZH - 1):
                @pl.when(k // 2 == i)
                def _():
                    send(zs.at[k], rsz.at[k], rsz_send.at[k], rsz_recv.at[k], z_peer[i])
            normed_grad(k)

        return carry

    lax.fori_loop(0, K + LS - 1, slot, 0)

    def own(h):
        k = KZ + h
        total = summed(k)
        for i in range(ZH - 1):
            wait(rsz.at[2 * i + h], rsz_recv.at[2 * i + h])
            total = total + rsz[2 * i + h].astype(F32)
        part[k, 0] = total.astype(BF)
        theirs = pl.ds(pl.multiple_of(o * C, C), C)
        fin[h] = part[k, 0, theirs, :]
        send(fin.at[h], finr.at[h], c_send.at[4 + h], c_recv.at[4 + h], partner)
        dw_ref[:, pl.ds(pl.multiple_of(c * 2 * C + h * C, C), C)] = part[k, 0, mine, :]

    wait_long(K - 1, LS - 1)
    wait_short(K - 1, SS - 1)
    weight(K - 1)
    own(0)
    normed_grad(K - 2)
    normed_grad(K - 1)
    dns[...] = acc[:, pl.ds(pl.multiple_of(o * C, C), C)].astype(BF)
    send(dns, dnr, c_send.at[6], c_recv.at[6], partner)
    own(1)
    wait(dnr, c_recv.at[6])
    dn_ref[...] = (acc[:, mine] + dnr[...].astype(F32)).astype(BF)
    for h in range(2):
        wait(finr.at[h], c_recv.at[4 + h])
        dw_ref[:, pl.ds(pl.multiple_of(o * 2 * C + h * C, C), C)] = finr[h]

    wait(og_par, c_send.at[0])
    for h in range(2):
        wait(fin.at[h], c_send.at[1 + h])
        wait(fin.at[h], c_send.at[4 + h])
    wait(nb.at[0], c_send.at[3])
    wait(dns, c_send.at[6])

    def drain(k, carry):
        wait(og.at[rows(0, 0, (ZL - 1) * 2 * R)], zl_send.at[k])
        wait(og.at[rows(0, 0, (Y - 1) * B)], y_send.at[k])
        wait(rsx.at[k], wx_send.at[k])
        wait(rsx.at[k], rsx_send.at[k])
        return carry

    def drain_z(k, carry):
        wait(zs.at[k], wz_send.at[k])
        wait(zs.at[k], rsz_send.at[k])
        return carry

    lax.fori_loop(0, K, drain, 0)
    lax.fori_loop(0, KZ, drain_z, 0)


def body(out_grad, normed, w_out):
    dma = pltpu.SemaphoreType.DMA
    vmem = pl.BlockSpec(memory_space=pltpu.VMEM)
    return pl.pallas_call(
        kernel,
        out_shape=(jax.ShapeDtypeStruct((RT, C), BF), jax.ShapeDtypeStruct((C, 4 * C), BF)),
        in_specs=[vmem] * 3,
        out_specs=(vmem, vmem),
        scratch_shapes=[
            pltpu.VMEM((R, ZH * X * 4 * C), BF),
            pltpu.VMEM((K * RT, W), BF),
            pltpu.VMEM((2, RT, C), BF),
            pltpu.VMEM((2 * C, RT), BF),
            pltpu.VMEM((K, X, 2 * C, C), BF),
            pltpu.VMEM((K, X, 2 * C, C), BF),
            pltpu.VMEM((K, X - 1, 2 * C, C), BF),
            pltpu.VMEM((KZ, 2 * C, C), BF),
            pltpu.VMEM((KZ, 2 * C, C), BF),
            pltpu.VMEM((2, C, C), BF),
            pltpu.VMEM((2, C, C), BF),
            pltpu.VMEM((RT, 2 * C), F32),
            pltpu.VMEM((RT, C), BF),
            pltpu.VMEM((RT, C), BF),
            dma((7,)), dma((7,)),
            dma((K,)), dma((K,)),
            dma((K,)), dma((K, LS + SS)),
            dma((KZ,)), dma((KZ,)),
            dma((K,)), dma((K,)),
            dma((K,)), dma((K,)),
            dma((KZ,)), dma((KZ,)),
        ],
        compiler_params=pltpu.CompilerParams(
            collective_id=0, has_side_effects=True, vmem_limit_bytes=40 * 1024 * 1024
        ),
        cost_estimate=pl.CostEstimate(flops=1_600_000_000, bytes_accessed=1_000_000, transcendentals=0),
    )(out_grad, normed, w_out)


def solution(mesh):
    in_specs = (P(("dp", "tensor"), None), P("dp", "tensor"), P("tensor", "dp"))
    out_specs = (P("dp", "tensor"), P("tensor", "dp"))
    return jax.shard_map(body, mesh=mesh, in_specs=in_specs, out_specs=out_specs, check_vma=False)
```

time: 411 us -> 78.8 us (0.19)
  the two profiles are of different devices: /device:TPU:1 before, /device:TPU:137 now
where the time goes in v1:
time: 78.8 us; the launch traced here: 78.6 us
  Pallas kernels  73.9 us (94%)
  local copies, waits for them, and re-layouts  4.01 us (5%)
    pallas_call x1, Pallas kernels, body(): pl.pallas_call(kernel, out_shape=(jax.ShapeDtypeStruct((RT, C), BF), jax....  73.9 us
    unnamed x8, local copies, waits for them, and re-layouts  4.01 us

profile of v1, /device:TPU:137, one launch (start us, length us, event | category | flops | bytes accessed | tf_op | source)
XLA Modules:
  0.0 78.6 jit_solution(18309604714276589939)
XLA Ops:
  0.6 0.0 copy-start
  0.6 0.9 %copy-done = bf16[512,128]{1,0:T(8,128)(2,1)S(1)} copy-done((bf16[512,128]{1,0:T(8,128)(2,1)S(1)}, bf16[512,128]{1,0:T(8,128)(2,1)}, u32[]{:S(2)}) %copy-start) | copy-done | bytes 131096
  1.5 0.0 copy-start.1
  1.5 0.9 %copy-done.1 = bf16[128,512]{1,0:T(8,128)(2,1)S(1)} copy-done((bf16[128,512]{1,0:T(8,128)(2,1)S(1)}, bf16[128,512]{1,0:T(8,128)(2,1)}, u32[]{:S(2)}) %copy-start.1) | copy-done | bytes 131096
  2.4 0.0 copy-start.2
  2.4 0.9 %copy-done.2 = bf16[8,6144]{1,0:T(8,128)(2,1)S(1)} copy-done((bf16[8,6144]{1,0:T(8,128)(2,1)S(1)}, bf16[8,6144]{1,0:T(8,128)(2,1)}, u32[]{:S(2)}) %copy-start.2) | copy-done | bytes 98328
  3.3 73.9 %shard_map.50 = (bf16[512,128]{1,0:T(8,128)(2,1)S(1)}, bf16[128,512]{1,0:T(8,128)(2,1)S(1)}) custom-call(bf16[8,6144]{1,0:T(8,128)(2,1)S(1)} %copy-done.2, bf16[512,128]{1,0:T(8,128)(2,1)S(1)} %copy-done, bf16[128,512]{1,0:T(8,128)(2,1)S(1)} %copy-done.1), custom_call_target="tpu_custom_call" | custom-call | flops 1600000000 | bytes 1000000 | tf_op jit(solution)/shard_map/pallas_call | solution.py:240
  77.2 0.7 copy.7
  77.9 0.7 copy.8
Async XLA Ops:
  0.6 0.9 %copy-start = (bf16[512,128]{1,0:T(8,128)(2,1)S(1)}, bf16[512,128]{1,0:T(8,128)(2,1)}, u32[]{:S(2)}) copy-start(bf16[512,128]{1,0:T(8,128)(2,1)} %n_ref.1) | copy-start | bytes 393220
  1.5 0.9 %copy-start.1 = (bf16[128,512]{1,0:T(8,128)(2,1)S(1)}, bf16[128,512]{1,0:T(8,128)(2,1)}, u32[]{:S(2)}) copy-start(bf16[128,512]{1,0:T(8,128)(2,1)} %w_ref.1) | copy-start | bytes 393220
  2.4 0.9 %copy-start.2 = (bf16[8,6144]{1,0:T(8,128)(2,1)S(1)}, bf16[8,6144]{1,0:T(8,128)(2,1)}, u32[]{:S(2)}) copy-start(bf16[8,6144]{1,0:T(8,128)(2,1)} %og_ref.1) | copy-start | bytes 294916

commit v2 on v0

v2 whole, which is shorter than its diff:
```python
import jax
import jax.numpy as jnp
from jax import lax
from jax.experimental import pallas as pl
from jax.experimental.pallas import tpu as pltpu
from jax.sharding import PartitionSpec as P

X, ZH, Y, ZL = 4, 3, 8, 4
R = 8
C = 128
W = 2 * C
OWN = ZH - 1
B = 2 * R * ZL
RT = B * Y
LS, SS = Y // 2, Y // 2 - 1
FAR, SIDES, TWICE, HERE = 0, 1, 2, 3
ORDER = [
    (0, FAR, 0), (1, FAR, 0), (0, SIDES, 0), (1, SIDES, 0), (0, FAR, 1), (1, FAR, 1),
    (0, SIDES, 1), (1, SIDES, 1), (2, TWICE, 0), (2, SIDES, 0), (2, SIDES, 1), (2, HERE, 0),
]
K = len(ORDER)
G_TABLE = sum(g << (2 * i) for i, (g, kind, h) in enumerate(ORDER))
KIND_TABLE = sum(kind << (2 * i) for i, (g, kind, h) in enumerate(ORDER))
H_TABLE = sum(h << i for i, (g, kind, h) in enumerate(ORDER))
Z_SLOTS = [(4, 0, 0), (5, 1, 0), (8, 0, 1), (9, 1, 1)]
GROUPS = [(0, 1), (1, 1), (2, 2), (4, 4), (8, 4)]
HOP = 3
LEAD = 1
W_START, W_OWN, W_Z, W_FAR, W_ALL = 7, 12, 17, 22, 25
NG_FROM, NG_RATE = 7, 3
MESH = pl.DeviceIdType.MESH
BF, F32 = jnp.bfloat16, jnp.float32


def pieces(kind, h):
    return {FAR: ((2, h), (0, h)), SIDES: ((1, h), (3, h)), TWICE: ((2, 0), (2, 1)), HERE: ((0, 0), (0, 1))}[kind]


def kernel(
    og_ref, n_ref, w_ref, dn_ref, dw_ref,
    og_own, og_par, og, nb, nt, w, part, kept, rsh, rsx, zs, rsz, fin, finr, acc, dns, dnr,
    own_sem, c_send, c_recv, zl_send, zl_recv, y_send, y_recv, wz_send, wz_recv, wx_send, wx_recv,
    rs_send, rsh_recv, rsx_recv, rsz_send, rsz_recv,
):
    dp, tn = lax.axis_index("dp"), lax.axis_index("tensor")
    zh, x = dp // X, dp % X
    y, zl, c = tn // (2 * ZL), (tn // 2) % ZL, tn % 2
    o = 1 - c
    partner = (dp, tn + 1 - 2 * c)
    zl_peer = [(dp, (y * ZL + (zl + j) % ZL) * 2 + c) for j in range(1, ZL)]
    z_peer = [(((zh + j) % ZH) * X + x, tn) for j in range(1, ZH)]
    x_up, x_down = (zh * X + (x + 1) % X, tn), (zh * X + (x + X - 1) % X, tn)

    def y_peer(sign):
        return (dp, (((y + sign + Y) % Y) * ZL + zl) * 2 + c)

    def send(src, dst, ssem, rsem, to):
        pltpu.make_async_remote_copy(
            src_ref=src, dst_ref=dst, send_sem=ssem, recv_sem=rsem, device_id=to, device_id_type=MESH
        ).start()

    def wait(ref, sem):
        pltpu.make_async_copy(ref, ref, sem).wait()

    mine, theirs = pl.ds(pl.multiple_of(c * C, C), C), pl.ds(pl.multiple_of(o * C, C), C)
    upper, lower = pl.ds(0, C), pl.ds(C, C)

    def half(of, h):
        return pl.ds(pl.multiple_of(of * W + h * C, C), C)

    stays = [
        pltpu.make_async_copy(og_ref, og_own, own_sem.at[0]),
        pltpu.make_async_copy(w_ref.at[:, half(c, 0)], w.at[OWN, 0, 0, mine], own_sem.at[1]),
        pltpu.make_async_copy(w_ref.at[:, half(c, 1)], w.at[OWN, 0, 1, mine], own_sem.at[2]),
        pltpu.make_async_copy(n_ref, nb.at[c], own_sem.at[3]),
    ]
    for copy in stays:
        copy.start()

    barrier = pltpu.get_barrier_semaphore()
    peers = [partner] + zl_peer + [x_up, x_down] + z_peer + [y_peer(1), y_peer(-1)]
    for peer in peers:
        pl.semaphore_signal(barrier, inc=1, device_id=peer, device_id_type=MESH)
    acc[...] = jnp.zeros_like(acc)
    pl.semaphore_wait(barrier, len(peers))

    send(og_ref, og_par, c_send.at[0], c_recv.at[0], partner)
    for h in range(2):
        send(w_ref.at[:, half(o, h)], w.at[OWN, 0, h, mine], c_send.at[5 + h], c_recv.at[5 + h], partner)
    send(n_ref, nb.at[c], c_send.at[2], c_recv.at[2], partner)

    slab = pl.ds(pl.multiple_of((y * ZL + zl) * 2 * R, 2 * R), 2 * R)
    stays[0].wait()
    wait(og_par, c_recv.at[0])
    for q, (first, number) in enumerate(GROUPS):
        for k in range(first, first + number):
            g, kind, h = ORDER[k]
            for i, (j, h) in enumerate(pieces(kind, h)):
                col = ((zh + 1 + g) % ZH * X + (x + j) % X) * 2 * W + c * W + h * C
                col = pl.ds(pl.multiple_of(col, C), C)
                a, b = og_own[:, col].astype(F32), og_par[:, col].astype(F32)
                top, low = jnp.where(c == 0, a, b), jnp.where(c == 0, b, a)
                og[k, slab, i * C : (i + 1) * C] = jnp.concatenate([top, low], axis=0).astype(BF)
        piece = og.at[pl.ds(first, number), slab]
        for peer in zl_peer:
            send(piece, piece, zl_send.at[q], zl_recv.at[q], peer)

    def w_start():
        for h in range(2):
            stays[1 + h].wait()
            wait(w.at[OWN, 0, h, theirs], c_recv.at[5 + h])
        w_near(OWN)
        for j in range(1, ZH):
            g = ZH - 1 - j
            send(w.at[OWN, 0], w.at[g, 0], wz_send.at[g], wz_recv.at[g], z_peer[j - 1])

    def w_near(g):
        send(w.at[g, 0], w.at[g, 3], wx_send.at[g, 0], wx_recv.at[g, 0], x_up)
        send(w.at[g, 0], w.at[g, 1], wx_send.at[g, 1], wx_recv.at[g, 1], x_down)

    def w_far(g):
        wait(w.at[g, 3], wx_recv.at[g, 0])
        send(w.at[g, 3, :, upper], w.at[g, 2, :, upper], wx_send.at[g, 2], wx_recv.at[g, 2], x_up)
        wait(w.at[g, 1], wx_recv.at[g, 1])
        send(w.at[g, 1, :, lower], w.at[g, 2, :, lower], wx_send.at[g, 3], wx_recv.at[g, 3], x_down)

    def block(k, at):
        return og.at[k, pl.ds(pl.multiple_of(((at + 2 * Y) % Y) * B, B), B)]

    def way(k):
        return 1 - 2 * (k % 2)

    def send_long(k, s):
        b = block(k, y - way(k) * s)
        send(b, b, y_send.at[k], y_recv.at[k, s], y_peer(way(k)))

    def send_short(k, s):
        b = block(k, y + way(k) * s)
        send(b, b, y_send.at[k], y_recv.at[k, LS + s], y_peer(-way(k)))

    def wait_long(k, s):
        wait(block(k, y - way(k) * (s + 1)), y_recv.at[k, s])

    def wait_short(k, s):
        wait(block(k, y + way(k) * (s + 1)), y_recv.at[k, LS + s])

    def begin(k):
        for q, (first, number) in enumerate(GROUPS):
            @pl.when(k == first)
            def _():
                wait(og.at[pl.ds(first, number), pl.ds(0, B - 2 * R)], zl_recv.at[q])

        send_long(k, 0)
        send_short(k, 0)

    def gathered(k):
        wait_long(k, LS - 1)
        wait_short(k, SS - 1)

    def chunk_weight(k):
        return jnp.dot(nt[...], og[k], preferred_element_type=F32)

    def x_sum(g, h, total):
        for i in range(2):
            wait(rsx.at[g, h, i], rsx_recv.at[g, h, i])
            total = total + rsx[g, h, i].astype(F32)
        return total

    def weight(k):
        g, kind, h = (G_TABLE >> (2 * k)) & 3, (KIND_TABLE >> (2 * k)) & 3, (H_TABLE >> k) & 1
        p = chunk_weight(k)

        def far(h):
            send(part.at[k, h, upper], rsh.at[g, h, 0], rs_send.at[g, h, 0], rsh_recv.at[g, h, 0], x_up)
            send(part.at[k, h, lower], rsh.at[g, h, 1], rs_send.at[g, h, 1], rsh_recv.at[g, h, 1], x_down)

        @pl.when(kind == FAR)
        def _():
            part[k, h] = p[:, :C].astype(BF)
            far(h)
            kept[g, h] = p[:, C:]

        @pl.when(kind == TWICE)
        def _():
            for i in range(2):
                part[k, i] = p[:, i * C : (i + 1) * C].astype(BF)
            for i in range(2):
                far(i)

        @pl.when(kind == SIDES)
        def _():
            wait(rsh.at[g, h, 0], rsh_recv.at[g, h, 0])
            part[k, 0, :C] = (p[:C, :C] + rsh[g, h, 0].astype(F32)).astype(BF)
            part[k, 0, C:] = p[C:, :C].astype(BF)
            send(part.at[k, 0], rsx.at[g, h, 0], rs_send.at[g, h, 2], rsx_recv.at[g, h, 0], x_up)
            wait(rsh.at[g, h, 1], rsh_recv.at[g, h, 1])
            part[k, 1, :C] = p[:C, C:].astype(BF)
            part[k, 1, C:] = (p[C:, C:] + rsh[g, h, 1].astype(F32)).astype(BF)
            send(part.at[k, 1], rsx.at[g, h, 1], rs_send.at[g, h, 3], rsx_recv.at[g, h, 1], x_down)

        for at, gz, hz in Z_SLOTS:
            @pl.when(k == at)
            def _():
                zs[gz, hz] = x_sum(gz, hz, kept[gz, hz]).astype(BF)
                send(zs.at[gz, hz], rsz.at[gz, hz], rsz_send.at[gz, hz], rsz_recv.at[gz, hz], z_peer[gz])

    def normed_grad(k, carry):
        g, kind, h = (G_TABLE >> (2 * k)) & 3, (KIND_TABLE >> (2 * k)) & 3, (H_TABLE >> k) & 1
        ja = jnp.where(kind == SIDES, 1, jnp.where(kind == HERE, 0, 2))
        jb = jnp.where(kind == SIDES, 3, jnp.where(kind == TWICE, 2, 0))
        hb = jnp.where(kind >= TWICE, 1, h)
        wk = jnp.concatenate([w[g, ja, h], w[g, jb, hb]], axis=1)
        acc[...] += lax.dot_general(og[k], wk, (((1,), (1,)), ((), ())), preferred_element_type=F32)
        return carry

    def normed_to(k):
        return jnp.clip(NG_RATE * (k - NG_FROM) + 2, 0, k + 1)

    for k in range(LEAD):
        begin(k)

    def slot(s, carry):
        @pl.when((s % 2 == 0) & (s // 2 + LEAD < K))
        def _():
            begin(s // 2 + LEAD)

        for i in range(1, LS):
            k = (s - HOP * i) // 2

            @pl.when((s >= HOP * i) & ((s - HOP * i) % 2 == 0) & (k < K))
            def _(i=i, k=k):
                wait_long(k, i - 1)
                send_long(k, i)
                if i < SS:
                    wait_short(k, i - 1)
                    send_short(k, i)

        @pl.when(s == HOP * LS - 1)
        def _():
            stays[3].wait()
            wait(nb.at[o], c_recv.at[2])
            for i in range(2):
                nt[i * C : (i + 1) * C, :] = nb[i].astype(F32).T.astype(BF)

        @pl.when(s == W_START)
        def _():
            w_start()

        @pl.when(s == W_OWN)
        def _():
            w_far(OWN)

        @pl.when(s == W_Z)
        def _():
            for g in range(OWN):
                wait(w.at[g, 0], wz_recv.at[g])
                w_near(g)

        @pl.when(s == W_FAR)
        def _():
            for g in range(OWN):
                w_far(g)

        @pl.when(s == W_ALL)
        def _():
            for g in range(ZH):
                wait(w.at[g, 2, :, upper], wx_recv.at[g, 2])
                wait(w.at[g, 2, :, lower], wx_recv.at[g, 3])

        @pl.when((s >= HOP * LS) & ((s - HOP * LS) % 2 == 0))
        def _():
            k = (s - HOP * LS) // 2
            gathered(k)
            weight(k)
            lax.fori_loop(normed_to(k - 1), normed_to(k), normed_grad, 0)

        return carry

    lax.fori_loop(0, 2 * (K - 1) + HOP * LS, slot, 0)

    gathered(K - 1)
    lax.fori_loop(normed_to(K - 2), K, normed_grad, 0)
    dns[...] = acc[:, theirs].astype(BF)
    send(dns, dnr, c_send.at[4], c_recv.at[4], partner)
    p = chunk_weight(K - 1)
    for h in range(2):
        total = x_sum(OWN, h, p[:, h * C : (h + 1) * C])
        for i in range(OWN):
            wait(rsz.at[i, h], rsz_recv.at[i, h])
            total = total + rsz[i, h].astype(F32)
        part[K - 1, h] = total.astype(BF)
        fin[:, h * C : (h + 1) * C] = part[K - 1, h, theirs, :]
    send(fin, finr, c_send.at[3], c_recv.at[3], partner)
    for h in range(2):
        dw_ref[:, half(c, h)] = part[K - 1, h, mine, :]
    wait(dnr, c_recv.at[4])
    dn_ref[...] = (acc[:, mine] + dnr[...].astype(F32)).astype(BF)

    wait(og_par, c_send.at[0])
    for h in range(2):
        wait(w.at[OWN, 0, h, mine], c_send.at[5 + h])
    wait(nb.at[0], c_send.at[2])
    wait(fin, c_send.at[3])
    wait(dns, c_send.at[4])
    for q, (first, number) in enumerate(GROUPS):
        wait(og.at[pl.ds(first, number), pl.ds(0, (ZL - 1) * 2 * R)], zl_send.at[q])
    for g in range(OWN):
        wait(w.at[g, 0], wz_send.at[g])
        for h in range(2):
            wait(zs.at[g, h], rsz_send.at[g, h])
    for g in range(ZH):
        wait(w.at[g, 3], wx_send.at[g, 0])
        wait(w.at[g, 1], wx_send.at[g, 1])
        wait(w.at[g, 2, :, upper], wx_send.at[g, 2])
        wait(w.at[g, 2, :, lower], wx_send.at[g, 3])

    for g in range(ZH):
        for h in range(2):
            for i in range(2):
                wait(rsh.at[g, h, i], rs_send.at[g, h, i])
                wait(rsx.at[g, h, i], rs_send.at[g, h, 2 + i])

    def drain(k, carry):
        wait(og.at[k, pl.ds(0, (Y - 1) * B)], y_send.at[k])
        return carry

    lax.fori_loop(0, K, drain, 0)
    wait(finr, c_recv.at[3])
    dw_ref[:, pl.ds(pl.multiple_of(o * W, W), W)] = finr[...]


def body(out_grad, normed, w_out):
    dma = pltpu.SemaphoreType.DMA
    vmem, hbm = pl.BlockSpec(memory_space=pltpu.VMEM), pl.BlockSpec(memory_space=pl.ANY)
    cols = ZH * X * 2 * W
    return pl.pallas_call(
        kernel,
        out_shape=(jax.ShapeDtypeStruct((RT, C), BF), jax.ShapeDtypeStruct((C, 2 * W), BF)),
        in_specs=[hbm] * 3,
        out_specs=(vmem, vmem),
        scratch_shapes=[
            pltpu.VMEM((R, cols), BF),
            pltpu.VMEM((R, cols), BF),
            pltpu.VMEM((K, RT, W), BF),
            pltpu.VMEM((2, RT, C), BF),
            pltpu.VMEM((2 * C, RT), BF),
            pltpu.VMEM((ZH, X, 2, 2 * C, C), BF),
            pltpu.VMEM((K, 2, 2 * C, C), BF),
            pltpu.VMEM((OWN, 2, 2 * C, C), F32),
            pltpu.VMEM((ZH, 2, 2, C, C), BF),
            pltpu.VMEM((ZH, 2, 2, 2 * C, C), BF),
            pltpu.VMEM((OWN, 2, 2 * C, C), BF),
            pltpu.VMEM((OWN, 2, 2 * C, C), BF),
            pltpu.VMEM((C, W), BF),
            pltpu.VMEM((C, W), BF),
            pltpu.VMEM((RT, 2 * C), F32),
            pltpu.VMEM((RT, C), BF),
            pltpu.VMEM((RT, C), BF),
            dma((4,)), dma((7,)), dma((7,)),
            dma((len(GROUPS),)), dma((len(GROUPS),)),
            dma((K,)), dma((K, LS + SS)),
            dma((OWN,)), dma((OWN,)),
            dma((ZH, 4)), dma((ZH, 4)),
            dma((ZH, 2, 4)), dma((ZH, 2, 2)), dma((ZH, 2, 2)),
            dma((OWN, 2)), dma((OWN, 2)),
        ],
        compiler_params=pltpu.CompilerParams(
            collective_id=0, has_side_effects=True, vmem_limit_bytes=56 * 1024 * 1024
        ),
        cost_estimate=pl.CostEstimate(flops=1_600_000_000, bytes_accessed=1_000_000, transcendentals=0),
    )(out_grad, normed, w_out)


def solution(mesh):
    in_specs = (P(("dp", "tensor"), None), P("dp", "tensor"), P("tensor", "dp"))
    out_specs = (P("dp", "tensor"), P("tensor", "dp"))
    return jax.shard_map(body, mesh=mesh, in_specs=in_specs, out_specs=out_specs, check_vma=False)
```

time: 411 us -> 76.4 us (0.19)
  waiting for transfers between devices: 387 us -> 0 us
  Pallas kernels: 0 us -> 73.3 us
  between operations: 13.8 us -> 0.65 us
  matrix products: 10.7 us -> 0 us
    all_gather x2 -> x0, waiting for transfers between devices: 218 us -> none  [the longest x1 136 us: body(): gathered = lax.all_gather(out_grad, 'tensor', axis=0, tiled=True)]
    reduce_scatter x1 -> x0, waiting for transfers between devices: 167 us -> none  [body(): lax.psum_scatter(d_weight.astype(jnp.bfloat16), 'dp', scatter_dimension=1...]
    pallas_call x0 -> x1, Pallas kernels: none -> 73.3 us  [body(): pl.pallas_call(kernel, out_shape=(jax.ShapeDtypeStruct((RT, C), BF), jax....]
    dot_general x2 -> x0, matrix products: 10.7 us -> none  [the longest x1 5.67 us: body(): lax.dot_general(gathered, w_full, (((1,), (1,)), ((), ())), preferred_ele...]
  transfers between devices with their start and end apart: 3 -> 0, of which waited for: 3 -> 0; matrix products, arithmetic and copies ran while one was open for 3% -> 0% of each run, Pallas kernels for 0% -> 0%
where the time goes in v2:
time: 76.4 us; the launch traced here: 76.3 us
  Pallas kernels  73.3 us (96%)
  local copies, waits for them, and re-layouts  2.26 us (3%)
    pallas_call x1, Pallas kernels, body(): pl.pallas_call(kernel, out_shape=(jax.ShapeDtypeStruct((RT, C), BF), jax....  73.3 us
    unnamed x4, local copies, waits for them, and re-layouts  2.26 us

profile of v2, /device:TPU:1, one launch (start us, length us, event | category | flops | bytes accessed | tf_op | source)
XLA Modules:
  0.0 76.3 jit_solution(12487345365448785313)
XLA Ops:
  0.6 73.3 %shard_map.50 = (bf16[512,128]{1,0:T(8,128)(2,1)}, bf16[128,512]{1,0:T(8,128)(2,1)}) custom-call(bf16[8,6144]{1,0:T(8,128)(2,1)} %og_ref.1, bf16[512,128]{1,0:T(8,128)(2,1)} %n_ref.1, bf16[128,512]{1,0:T(8,128)(2,1)} %w_ref.1), custom_call_target="tpu_custom_call" | custom-call | flops 1600000000 | bytes 1000000 | tf_op jit(solution)/shard_map/pallas_call | solution.py:336
  74.0 0.0 copy-start
  74.0 1.6 %copy.7 = bf16[512,128]{1,0:T(8,128)(2,1)} copy(bf16[512,128]{1,0:T(8,128)(2,1)} %get-tuple-element.4) | data formatting | bytes 262144
  75.6 0.0 copy-done
  75.6 0.7 copy.8
Async XLA Ops:
  74.0 1.6 %copy-start = (bf16[128,512]{1,0:T(8,128)(2,1)S(1)}, bf16[128,512]{1,0:T(8,128)(2,1)}, u32[]{:S(2)}) copy-start(bf16[128,512]{1,0:T(8,128)(2,1)} %get-tuple-element.5) | copy-start | bytes 393220

commit v3 on v2

--- a/solution.py
+++ b/solution.py
@@ -365,10 +365,10 @@
             dma((OWN, 2)), dma((OWN, 2)),
         ],
         compiler_params=pltpu.CompilerParams(
-            collective_id=0, has_side_effects=True, vmem_limit_bytes=56 * 1024 * 1024
+            collective_id=0, has_side_effects=True, vmem_limit_bytes=44 * 1024 * 1024
         ),
         cost_estimate=pl.CostEstimate(flops=1_600_000_000, bytes_accessed=1_000_000, transcendentals=0),
-    )(out_grad, normed, w_out)
+    )(*(pltpu.with_memory_space_constraint(a, pltpu.HBM) for a in (out_grad, normed, w_out)))
 
 
 def solution(mesh):

time: 76.4 us -> 74.7 us (0.978)
  local copies, waits for them, and re-layouts: 2.26 us -> 1.31 us
    unnamed x4 -> x2, local copies, waits for them, and re-layouts: 2.26 us -> 1.31 us
where the time goes in v3:
time: 74.7 us; the launch traced here: 74.6 us
  Pallas kernels  72.7 us (97%)
  local copies, waits for them, and re-layouts  1.31 us (2%)
    pallas_call x1, Pallas kernels, body(): pl.pallas_call(kernel, out_shape=(jax.ShapeDtypeStruct((RT, C), BF), jax....  72.7 us

profile of v3, /device:TPU:1, one launch (start us, length us, event | category | flops | bytes accessed | tf_op | source)
XLA Modules:
  0.0 74.6 jit_solution(12727406102971901239)
XLA Ops:
  0.6 72.7 %shard_map.50 = (bf16[512,128]{1,0:T(8,128)(2,1)S(1)}, bf16[128,512]{1,0:T(8,128)(2,1)S(1)}) custom-call(bf16[8,6144]{1,0:T(8,128)(2,1)} %og_ref.1, bf16[512,128]{1,0:T(8,128)(2,1)} %n_ref.1, bf16[128,512]{1,0:T(8,128)(2,1)} %w_ref.1), custom_call_target="tpu_custom_call" | custom-call | flops 1600000000 | bytes 1000000 | tf_op jit(solution)/shard_map/pallas_call | solution.py:336
  73.3 0.7 copy.7
  74.0 0.7 copy.8

commit v4 on v3

--- a/solution.py
+++ b/solution.py
@@ -214,12 +214,12 @@
         return carry
 
     def normed_to(k):
-        return jnp.clip(NG_RATE * (k - NG_FROM) + 2, 0, k + 1)
+        return min(max(NG_RATE * (k - NG_FROM) + 2, 0), k + 1)
 
     for k in range(LEAD):
         begin(k)
 
-    def slot(s, carry):
+    def slot(s):
         @pl.when((s % 2 == 0) & (s // 2 + LEAD < K))
         def _():
             begin(s // 2 + LEAD)
@@ -274,9 +274,8 @@
             weight(k)
             lax.fori_loop(normed_to(k - 1), normed_to(k), normed_grad, 0)
 
-        return carry
-
-    lax.fori_loop(0, 2 * (K - 1) + HOP * LS, slot, 0)
+    for s in range(2 * (K - 1) + HOP * LS):
+        slot(s)
 
     gathered(K - 1)
     lax.fori_loop(normed_to(K - 2), K, normed_grad, 0)

time: 74.7 us -> 74.4 us (level)
  no operation moved by 1% of the time
where the time goes in v4:
time: 74.4 us; the launch traced here: 74.2 us
  Pallas kernels  72.3 us (97%)
  local copies, waits for them, and re-layouts  1.31 us (2%)
    pallas_call x1, Pallas kernels, body(): pl.pallas_call(kernel, out_shape=(jax.ShapeDtypeStruct((RT, C), BF), jax....  72.3 us

profile of v4, /device:TPU:1, one launch (start us, length us, event | category | flops | bytes accessed | tf_op | source)
XLA Modules:
  0.0 74.2 jit_solution(11971010914148251055)
XLA Ops:
  0.6 72.3 %shard_map.50 = (bf16[512,128]{1,0:T(8,128)(2,1)S(1)}, bf16[128,512]{1,0:T(8,128)(2,1)S(1)}) custom-call(bf16[8,6144]{1,0:T(8,128)(2,1)} %og_ref.1, bf16[512,128]{1,0:T(8,128)(2,1)} %n_ref.1, bf16[128,512]{1,0:T(8,128)(2,1)} %w_ref.1), custom_call_target="tpu_custom_call" | custom-call | flops 1600000000 | bytes 1000000 | tf_op jit(solution)/shard_map/pallas_call | solution.py:335
  72.9 0.7 copy.7
  73.6 0.7 copy.8

commit v5 on v4

--- a/solution.py
+++ b/solution.py
@@ -25,7 +25,7 @@
 Z_SLOTS = [(4, 0, 0), (5, 1, 0), (8, 0, 1), (9, 1, 1)]
 GROUPS = [(0, 1), (1, 1), (2, 2), (4, 4), (8, 4)]
 HOP = 3
-LEAD = 1
+LEAD = 2
 W_START, W_OWN, W_Z, W_FAR, W_ALL = 7, 12, 17, 22, 25
 NG_FROM, NG_RATE = 7, 3
 MESH = pl.DeviceIdType.MESH

time: 74.4 us -> 73 us (0.981)
  Pallas kernels: 72.3 us -> 70.9 us
    pallas_call x1, Pallas kernels: 72.3 us -> 70.9 us  [body(): pl.pallas_call(kernel, out_shape=(jax.ShapeDtypeStruct((RT, C), BF), jax....]
where the time goes in v5:
time: 73 us; the launch traced here: 72.9 us
  Pallas kernels  70.9 us (97%)
  local copies, waits for them, and re-layouts  1.31 us (2%)
    pallas_call x1, Pallas kernels, body(): pl.pallas_call(kernel, out_shape=(jax.ShapeDtypeStruct((RT, C), BF), jax....  70.9 us

profile of v5, /device:TPU:1, one launch (start us, length us, event | category | flops | bytes accessed | tf_op | source)
XLA Modules:
  0.0 72.9 jit_solution(5345291777602244689)
XLA Ops:
  0.6 70.9 %shard_map.50 = (bf16[512,128]{1,0:T(8,128)(2,1)S(1)}, bf16[128,512]{1,0:T(8,128)(2,1)S(1)}) custom-call(bf16[8,6144]{1,0:T(8,128)(2,1)} %og_ref.1, bf16[512,128]{1,0:T(8,128)(2,1)} %n_ref.1, bf16[128,512]{1,0:T(8,128)(2,1)} %w_ref.1), custom_call_target="tpu_custom_call" | custom-call | flops 1600000000 | bytes 1000000 | tf_op jit(solution)/shard_map/pallas_call | solution.py:335
  71.5 0.7 copy.7
  72.2 0.7 copy.8
